TPU v7x, 32 devices: a whole 2x2x4 slice. The times are simulated.
32 devices in a mesh: wide: 8 (over z, y), sub: 4 (over x, core).
Axes of the slice: x: 2, y: 2, z: 4, core: 2. Of those that a mesh axis runs over, the one named last changes fastest.
Arguments:
- lengths: int32 [4, 1024], P('sub', 'wide'), may hold values from 0 to 2048, as said below
- postings: bfloat16 [4, 16384, 128], P('sub', 'wide'), may hold values from -6 to 6
- codes: int32 [4, 8, 16384], P('sub', None, 'wide'), may hold values from 0 to 255
- rotation: bfloat16 [128, 128], replicated, may hold values from -0.5 to 0.5
Outputs:
- rotated_slices: bfloat16 [4, 128, 8192], P(None, 'sub', 'wide')
- codebook: float32 [8, 16, 256], P('sub')
Inputs may be any that keep to these rules, and one draw needn't show every extreme that they name: Each slab's lengths add up to 8192; no device holds more than 2048 rows in all; in each slab some device holds exactly 2048 rows, all in one list; lengths and whole devices may be empty.
All inputs are finite; a program needn't handle non-finite values.
Results may differ from a plain program's by a relative error of at most 0.0029.
Values may be sent and summed in bfloat16 or wider, within the bound.
A program may use at most 128 MiB of HBM per device.

v0:
```python
import jax
import jax.numpy as jnp
from jax import lax
from jax.sharding import PartitionSpec as P

KCODES = 256
SUBDIM = 16


def entering(part, axis, combine, identity):
    place = lax.axis_index(axis)
    gathered = lax.all_gather(part, axis)
    state = jnp.zeros_like(part) + jnp.asarray(identity, part.dtype)

    def one(turn, state):
        return combine(state, lax.dynamic_index_in_dim(gathered, turn, 0, False))

    return lax.fori_loop(0, place, one, state)


def add_counts(earlier, later):
    return earlier + later


def body(lengths, postings, codes, rotation):
    here = lax.axis_index("wide")
    capacity = postings.shape[1]
    per_shard = capacity // 2
    total = jnp.sum(lengths)
    offset = entering(total, "wide", add_counts, jnp.int32(0))
    marks = jnp.stack([offset, total]).astype(jnp.int32).reshape(1, 1, 2)
    code_rows = jnp.swapaxes(codes, 1, 2)
    targets = here * per_shard + jnp.arange(per_shard, dtype=jnp.int32)

    def place(carry, pieces, start):
        rows_piece, code_piece, mark_piece = pieces
        shards = mark_piece.shape[1]
        slots = rows_piece.shape[1] // shards

        def one_shard(shard, state):
            rows_acc, code_acc = state
            block_rows = lax.dynamic_slice_in_dim(rows_piece[0], shard * slots, slots, 0)
            block_codes = lax.dynamic_slice_in_dim(code_piece[0], shard * slots, slots, 0)
            source_start = mark_piece[0, shard, 0]
            source_total = mark_piece[0, shard, 1]
            within = targets - source_start
            usable = (within >= 0) & (within < source_total)
            safe = jnp.clip(within, 0, slots - 1)
            rows_acc = jnp.where(usable[:, None], jnp.take(block_rows, safe, axis=0), rows_acc)
            code_acc = jnp.where(usable[:, None], jnp.take(block_codes, safe, axis=0), code_acc)
            return (rows_acc, code_acc)

        return lax.fori_loop(0, shards, one_shard, carry)

    start_rows = jnp.zeros((per_shard, postings.shape[2]), jnp.bfloat16)
    start_codes = jnp.zeros((per_shard, codes.shape[1]), jnp.int32)
    kept, kept_code_rows = place(
        (start_rows, start_codes),
        (
            lax.all_gather(postings, "wide", axis=1, tiled=True),
            lax.all_gather(code_rows, "wide", axis=1, tiled=True),
            lax.all_gather(marks, "wide", axis=1, tiled=True),
        ),
        jnp.int32(0),
    )
    kept_codes = kept_code_rows.T
    rotated = jnp.einsum("rd,de->er", kept, rotation, preferred_element_type=jnp.float32).astype(
        jnp.bfloat16
    )
    slices, slice_codes = (
        lax.all_to_all(rotated[None], "sub", split_axis=1, concat_axis=0, tiled=True),
        lax.all_to_all(kept_codes[None], "sub", split_axis=1, concat_axis=0, tiled=True),
    )
    local_count = slice_codes.shape[1]
    centroid_ids = jnp.arange(KCODES, dtype=jnp.int32)
    sum_list = []
    count_list = []
    for local in range(local_count):
        values = slices[:, local * SUBDIM : (local + 1) * SUBDIM, :]
        onehot = (slice_codes[:, local, :, None] == centroid_ids).astype(jnp.bfloat16)
        sum_list.append(
            jnp.einsum("gde,gek->dk", values, onehot, preferred_element_type=jnp.float32)
        )
        count_list.append(jnp.sum(onehot.astype(jnp.float32), axis=(0, 1)))
    partial_sums = jnp.stack(sum_list)
    partial_counts = jnp.stack(count_list)
    full_sums, full_counts = lax.psum((partial_sums, partial_counts), "wide")
    codebook = full_sums / (full_counts[:, None, :] + 1.0)
    return (slices, codebook)


def solution(mesh):
    return jax.shard_map(
        body,
        mesh=mesh,
        in_specs=(P("sub", "wide"), P("sub", "wide", None), P("sub", None, "wide"), P()),
        out_specs=(P(None, "sub", "wide"), P("sub", None, None)),
        check_vma=False,
    )
```

profile of v0, /device:TPU:0, one launch (start us, length us, event | category | flops | bytes accessed | tf_op | source)
XLA Modules:
  0.0 384.8 jit_solution(17787069196864160257)
XLA Ops:
  10.5 1.4 dynamic-update-slice
  11.9 13.2 %all-reduce = s32[8]{0:T(128)S(1)} all-reduce(s32[8]{0:T(128)S(1)} %dynamic-update-slice), channel_id=1, replica_groups=mesh['wide'=8,'sub'=4] {'wide'}, use_global_device_ids=true, to_apply=%add | all-reduce | flops 8 | bytes 64
  26.5 15.9 %all-reduce.1 = s32[16]{0:T(128)S(1)} all-reduce(s32[16]{0:T(128)S(1)} %add_dynamic-update-slice_fusion), channel_id=2, replica_groups=mesh['wide'=8,'sub'=4] {'wide'}, use_global_device_ids=true, to_apply=%add.1 | all-reduce | flops 16 | bytes 128
  43.8 179.0 %all_gather.19 = s32[1,16384,8]{2,1,0:T(8,128)} all-gather(s32[1,2048,8]{2,1,0:T(8,128)S(1)} %bitcast.50), channel_id=1, replica_groups=mesh['wide'=8,'sub'=4] {'wide'}, dimensions={1}, use_global_device_ids=true | all-gather | bytes 589824 | tf_op jit(solution)/shard_map/all_gather | solution.py:61
  222.8 96.4 %while.27 = (s32[]{:T(128)}, bf16[1024,128]{1,0:T(8,128)(2,1)S(1)}, s32[1024,8]{1,0:T(8,128)S(1)}, s32[1,8,2]{1,2,0:T(2,128)S(1)}, bf16[1,16384,128]{2,1,0:T(8,1...) while((s32[]{:T(128)}, bf16[1024,128]{1,0:T(8,128)(2,1)S(1)}, ...), condition=%wide.region_4.5_spmd.clone, body=%wide.region_3.4_spmd.clone.sunk | while | flops 437255 | bytes 2689238 | solution.py:53
  225.4 2.8 gather_fusion.1
  231.1 3.2 gather_fusion
  234.8 1.3 dynamic-slice_bitcast_fusion.5
  237.5 2.8 gather_fusion.1
  243.2 3.2 gather_fusion
  246.9 1.3 dynamic-slice_bitcast_fusion.5
  249.5 2.8 gather_fusion.1
  255.2 3.2 gather_fusion
  258.9 1.3 dynamic-slice_bitcast_fusion.5
  261.6 2.8 gather_fusion.1
  267.3 3.2 gather_fusion
  271.0 1.3 dynamic-slice_bitcast_fusion.5
  273.6 2.8 gather_fusion.1
  279.3 3.2 gather_fusion
  285.7 2.8 gather_fusion.1
  291.4 3.2 gather_fusion
  297.7 2.8 gather_fusion.1
  303.4 3.2 gather_fusion
  309.8 2.8 gather_fusion.1
  315.5 3.2 gather_fusion
  320.0 3.3 all-to-all-start.1
  324.5 2.1 reduce.1
  327.5 3.4 all-to-all-start
  332.7 4.2 %all-to-all-done = bf16[4,2,16384]{2,1,0:T(2,128)(2,1)S(1)} async-done(((bf16[4,2,16384]{2,1,0:T(2,128)(2,1)}), bf16[4,2,16384]{2,1,0:T(2,128)(2,1)S(1)}, u32[]{:S(2)}, u32[]{:S(2)}) %all-to-all-start) | async-done | bytes 262176 | tf_op jit(solution)/shard_map/all_to_all | solution.py:71
  337.3 1.4 fusion.13
  338.7 1.4 fusion.14
  340.1 37.2 %all-reduce.2 = (f32[2,16,256]{2,1,0:T(8,128)S(1)}, f32[2,256]{1,0:T(2,128)S(1)}) all-reduce(f32[2,16,256]{2,1,0:T(8,128)S(1)} %pad_maximum_fusion, f32[2,256]{1,0:T(2,128)S(1)} %pad_maximum_fusion.1), channel_id=1, replica_groups=mesh['wide'=8,'sub'=4] {'wide'}, use_global_device_ids=true, to_apply=%region_5.6 | all-reduce | flops 8704 | bytes 69632 | tf_op jit(solution)/shard_map/psum | solution.py:87
  (105 shorter events, 53.6 us)
Async XLA Ops:
  7.2 316.1 %copy-start = (bf16[128,128]{1,0:T(8,128)(2,1)S(1)}, bf16[128,128]{1,0:T(8,128)(2,1)}, u32[]{:S(2)}) copy-start(bf16[128,128]{1,0:T(8,128)(2,1)} %param.11) | copy-start | bytes 98308
  7.2 215.6 %all-gather.3.cloned.1.call-start = ((), (), s32[]{:S(2)}) async-start(), calls=%async_computation.2 | async-start | bytes 4718592 | tf_op jit(solution)/shard_map/all_gather | solution.py:60
  320.0 7.6 %all-to-all-start.1 = ((s32[1,8,1024]{2,0,1:T(1,128)}), s32[1,8,1024]{2,0,1:T(1,128)S(1)}, u32[]{:S(2)}, u32[]{:S(2)}) async-start(s32[1,8,1024]{2,0,1:T(1,128)} %broadcast_in_dim.90), calls=%async_computation.1 | async-start | bytes 65536 | tf_op jit(solution)/shard_map/all_to_all | solution.py:72
  327.5 9.4 %all-to-all-start = ((bf16[4,2,16384]{2,1,0:T(2,128)(2,1)}), bf16[4,2,16384]{2,1,0:T(2,128)(2,1)S(1)}, u32[]{:S(2)}, u32[]{:S(2)}) async-start(bf16[4,2,16384]{2,1,0:T(2,128)(2,1)} %reshape.97), calls=%async_computation | async-start | bytes 524288 | tf_op jit(solution)/shard_map/all_to_all | solution.py:71
  337.3 40.7 %copy-start.1 = (bf16[1,128,1024]{2,1,0:T(8,128)(2,1)}, bf16[1,128,1024]{2,1,0:T(8,128)(2,1)S(1)}, u32[]{:S(2)}) copy-start(bf16[1,128,1024]{2,1,0:T(8,128)(2,1)S(1)} %copy.21) | copy-start | bytes 786436
Sparse Core Ops, SparseCore 0:
  10.1 137.8 all-gather.2
where the time goes:
time: 386 us; the launch traced here: 385 us
  blocking collectives  245 us (63%)
  local copies, waits for them, and re-layouts  79.5 us (21%)
  other arithmetic  30 us (8%)
  between operations  14.8 us (4%)
  starting transfers between devices  6.71 us (2%)
  waiting for transfers between devices  4.89 us (1%)
    all_gather x1, blocking collectives, body(): lax.all_gather(code_rows, 'wide', axis=1, tiled=True)  179 us
    psum x1, blocking collectives, body(): full_sums, full_counts = lax.psum((partial_sums, partial_counts), 'wide')  37.2 us
    unnamed x2, blocking collectives  29.1 us
    gather x8, local copies, waits for them, and re-layouts, one_shard(): jnp.take(block_rows, safe, axis=0)  25.6 us
    gather x8, local copies, waits for them, and re-layouts, one_shard(): jnp.take(block_codes, safe, axis=0)  22.5 us
    dynamic_slice x8, local copies, waits for them, and re-layouts, one_shard(): lax.dynamic_slice_in_dim(code_piece[0], shard * slots, slots, 0)  10.4 us
    and x8, other arithmetic, one_shard(): usable = (within >= 0) & (within < source_total)  10.3 us
    dynamic_slice x8, local copies, waits for them, and re-layouts, one_shard(): lax.dynamic_slice_in_dim(rows_piece[0], shard * slots, slots, 0)  8.67 us
  transfers between devices with their start and end apart: 3, of which 1 were waited for; matrix products, arithmetic and copies ran while one was open for 3% of the time, Pallas kernels for 0%

commit v1 on v0

--- a/solution.py
+++ b/solution.py
@@ -5,6 +5,27 @@
 
 KCODES = 256
 SUBDIM = 16
+
+
+def gather_around(value, axis, dim):
+    length, position, span = (lax.axis_size(axis), lax.axis_index(axis), value.shape[dim])
+    upward = [(i, (i + 1) % length) for i in range(length)]
+    left = [(i, (i - 1) % length) for i in range(length)]
+    out = jnp.zeros((*value.shape[:dim], length * span, *value.shape[dim + 1 :]), value.dtype)
+    out = lax.dynamic_update_slice_in_dim(out, value, position * span, axis=dim)
+    from_left = from_right = value
+    half = length // 2
+    for step in range(1, half + 1):
+        from_left = lax.ppermute(from_left, axis, upward)
+        out = lax.dynamic_update_slice_in_dim(
+            out, from_left, (position - step) % length * span, axis=dim
+        )
+        if step < length - half:
+            from_right = lax.ppermute(from_right, axis, left)
+            out = lax.dynamic_update_slice_in_dim(
+                out, from_right, (position + step) % length * span, axis=dim
+            )
+    return out
 
 
 def entering(part, axis, combine, identity):
@@ -58,7 +79,7 @@
         (start_rows, start_codes),
         (
             lax.all_gather(postings, "wide", axis=1, tiled=True),
-            lax.all_gather(code_rows, "wide", axis=1, tiled=True),
+            gather_around(code_rows, "wide", 1),
             lax.all_gather(marks, "wide", axis=1, tiled=True),
         ),
         jnp.int32(0),

time: 386 us -> 254 us (0.66)
  blocking collectives: 245 us -> 63.2 us
  waiting for transfers between devices: 4.89 us -> 25 us
  starting transfers between devices: 6.71 us -> 22.5 us
  local copies, waits for them, and re-layouts: 79.5 us -> 93.8 us
    all_gather x1 -> x0, blocking collectives: 179 us -> none  [body(): lax.all_gather(code_rows, 'wide', axis=1, tiled=True)]
    ppermute x0 -> x7, starting transfers between devices: none -> 15.8 us  [the longest x3 11.3 us: gather_around(): from_right = lax.ppermute(from_right, axis, left)]
    all_gather x1, waiting for transfers between devices: 0.01 us -> 12.5 us  [body(): lax.all_gather(postings, 'wide', axis=1, tiled=True)]
    dynamic_update_slice x0 -> x8, local copies, waits for them, and re-layouts: none -> 8.51 us  [the longest x4 4.25 us: gather_around(): lax.dynamic_update_slice_in_dim(out, from_left, (position - step) % lengt...]
    ppermute x0 -> x7, waiting for transfers between devices: none -> 7.62 us  [the longest x4 7.62 us: gather_around(): from_left = lax.ppermute(from_left, axis, upward)]
  transfers between devices with their start and end apart: 3 -> 10, of which waited for: 1 -> 5; matrix products, arithmetic and copies ran while one was open for 3% -> 10% of each run, Pallas kernels for 0% -> 0%
where the time goes in v1:
time: 254 us; the launch traced here: 253 us
  local copies, waits for them, and re-layouts  93.8 us (37%)
  blocking collectives  63.2 us (25%)
  other arithmetic  30 us (12%)
  waiting for transfers between devices  25 us (10%)
  starting transfers between devices  22.5 us (9%)
  between operations  14.9 us (6%)
  matrix products  2.98 us (1%)
    psum x1, blocking collectives, body(): full_sums, full_counts = lax.psum((partial_sums, partial_counts), 'wide')  34.7 us
    unnamed x2, blocking collectives  28.5 us
    gather x8, local copies, waits for them, and re-layouts, one_shard(): jnp.take(block_rows, safe, axis=0)  25.6 us
    gather x8, local copies, waits for them, and re-layouts, one_shard(): jnp.take(block_codes, safe, axis=0)  22.5 us
    all_gather x1, waiting for transfers between devices, body(): lax.all_gather(postings, 'wide', axis=1, tiled=True)  12.5 us
    ppermute x3, starting transfers between devices, gather_around(): from_right = lax.ppermute(from_right, axis, left)  11.3 us
    dynamic_slice x8, local copies, waits for them, and re-layouts, one_shard(): lax.dynamic_slice_in_dim(code_piece[0], shard * slots, slots, 0)  10.4 us
    and x8, other arithmetic, one_shard(): usable = (within >= 0) & (within < source_total)  10.3 us
  transfers between devices with their start and end apart: 10, of which 5 were waited for; matrix products, arithmetic and copies ran while one was open for 10% of the time, Pallas kernels for 0%

profile of v1, /device:TPU:0, one launch (start us, length us, event | category | flops | bytes accessed | tf_op | source)
XLA Modules:
  0.0 253.1 jit_solution(4811425691137207825)
XLA Ops:
  7.9 3.0 %collective-permute-start = (s32[1,2048,8]{1,2,0:T(8,128)}, s32[1,2048,8]{1,2,0:T(8,128)S(1)}, u32[]{:S(2)}, u32[]{:S(2)}) collective-permute-start(s32[1,2048,8]{1,2,0:T(8,128)} %bitcast.58), channel_id=1, source_target_pairs={{0,4},{4,8},{8,12},{12,16},{16,20},{20,24},{24,28},{28,0},{1,5},{5... | collective-permute-start | bytes 196616 | tf_op jit(solution)/shard_map/ppermute | solution.py:19
  14.9 3.1 %collective-permute-start.1 = (s32[1,2048,8]{1,2,0:T(8,128)}, s32[1,2048,8]{1,2,0:T(8,128)S(1)}, u32[]{:S(2)}, u32[]{:S(2)}) collective-permute-start(s32[1,2048,8]{1,2,0:T(8,128)} %bitcast.59), channel_id=1, source_target_pairs={{0,28},{4,0},{8,4},{12,8},{16,12},{20,16},{24,20},{28,24},{1,29},{... | collective-permute-start | bytes 196616 | tf_op jit(solution)/shard_map/ppermute | solution.py:24
  17.9 10.1 %all-reduce = s32[8]{0:T(128)S(1)} all-reduce(s32[8]{0:T(128)S(1)} %dynamic-update-slice), channel_id=1, replica_groups=mesh['wide'=8,'sub'=4] {'wide'}, use_global_device_ids=true, to_apply=%add | all-reduce | flops 8 | bytes 64
  30.7 3.5 %broadcast_in_dim.92 = s32[1,16384,8]{2,1,0:T(8,128)} broadcast(s32[]{:T(128)} %constant.146.clone.1), dimensions={} | broadcast | bytes 524292 | tf_op jit(solution)/shard_map/broadcast_in_dim | solution.py:14
  35.3 18.4 %all-reduce.1 = s32[16]{0:T(128)S(1)} all-reduce(s32[16]{0:T(128)S(1)} %add_dynamic-update-slice_fusion), channel_id=2, replica_groups=mesh['wide'=8,'sub'=4] {'wide'}, use_global_device_ids=true, to_apply=%add.1 | all-reduce | flops 16 | bytes 128
  55.9 3.5 %collective-permute-start.3 = (s32[1,2048,8]{1,2,0:T(8,128)S(1)}, s32[1,2048,8]{1,2,0:T(8,128)S(1)}, u32[]{:S(2)}, u32[]{:S(2)}) collective-permute-start(s32[1,2048,8]{1,2,0:T(8,128)S(1)} %collective-permute-done.1), channel_id=1, source_target_pairs={{0,28},{4,0},{8,4},{12,8},{16,12},{20,16},{24,20},{28,24},{1,29},{... | collective-permute-start | bytes 196616 | tf_op jit(solution)/shard_map/ppermute | solution.py:24
  61.5 1.6 collective-permute-done.2
  63.9 4.8 %collective-permute-start.5 = (s32[1,2048,8]{1,2,0:T(8,128)S(1)}, s32[1,2048,8]{1,2,0:T(8,128)S(1)}, u32[]{:S(2)}, u32[]{:S(2)}) collective-permute-start(s32[1,2048,8]{1,2,0:T(8,128)S(1)} %collective-permute-done.3), channel_id=1, source_target_pairs={{0,28},{4,0},{8,4},{12,8},{16,12},{20,16},{24,20},{28,24},{1,29},{... | collective-permute-start | bytes 196616 | tf_op jit(solution)/shard_map/ppermute | solution.py:24
  75.2 4.5 %collective-permute-done.6 = s32[1,2048,8]{1,2,0:T(8,128)S(1)} collective-permute-done((s32[1,2048,8]{1,2,0:T(8,128)S(1)}, s32[1,2048,8]{1,2,0:T(8,128)S(1)}, u32[]{:S(2)}, u32[]{:S(2)}) %collective-permute-start.6) | collective-permute-done | bytes 65568 | tf_op jit(solution)/shard_map/ppermute | solution.py:19
  81.0 12.5 %all-gather.3.cloned.1.call-done = bf16[1,16384,128]{2,1,0:T(8,128)(2,1)} async-done(((bf16[1,2048,128]{2,1,0:T(8,128)(2,1)}), bf16[1,16384,128]{2,1,0:T(8,128)(2,1)}) %all-gather.3.cloned.1.call-update) | async-done | bytes 4194320 | tf_op jit(solution)/shard_map/all_gather | solution.py:81
  93.5 96.4 %while.27 = (s32[]{:T(128)}, bf16[1024,128]{1,0:T(8,128)(2,1)S(1)}, s32[1024,8]{1,0:T(8,128)S(1)}, s32[1,8,2]{1,2,0:T(2,128)S(1)}, bf16[1,16384,128]{2,1,0:T(8,1...) while((s32[]{:T(128)}, bf16[1024,128]{1,0:T(8,128)(2,1)S(1)}, ...), condition=%wide.region_4.5_spmd.clone, body=%wide.region_3.4_spmd.clone.sunk | while | flops 437255 | bytes 2689238 | solution.py:74
  96.2 2.8 %gather_fusion.1 = s32[1024,8]{1,0:T(8,128)S(1)} fusion(s32[2048,8]{1,0:T(8,128)S(1)} %dynamic-slice_bitcast_fusion.5, s32[1024]{0:T(1024)S(1)} %broadcast_clamp_fusion.2), kind=kCustom, calls=%fused_computation.1.clone.clone.1 | custom fusion | bytes 69632 | tf_op jit(solution)/shard_map/while/body/eval_jaxpr/jit(_take)/gather | solution.py:71
  101.9 3.2 %gather_fusion = bf16[1024,128]{1,0:T(8,128)(2,1)S(1)} fusion(bf16[2048,128]{1,0:T(8,128)(2,1)S(1)} %dynamic-slice_bitcast_fusion.4, s32[1024]{0:T(1024)S(1)} %broadcast_clamp_fusion.2), kind=kCustom, calls=%fused_computation.clone.clone.1 | custom fusion | bytes 528384 | tf_op jit(solution)/shard_map/while/body/eval_jaxpr/jit(_take)/gather | solution.py:70
  108.2 2.8 %gather_fusion.1 = s32[1024,8]{1,0:T(8,128)S(1)} fusion(s32[2048,8]{1,0:T(8,128)S(1)} %dynamic-slice_bitcast_fusion.5, s32[1024]{0:T(1024)S(1)} %broadcast_clamp_fusion.2), kind=kCustom, calls=%fused_computation.1.clone.clone.1 | custom fusion | bytes 69632 | tf_op jit(solution)/shard_map/while/body/eval_jaxpr/jit(_take)/gather | solution.py:71
  113.9 3.2 %gather_fusion = bf16[1024,128]{1,0:T(8,128)(2,1)S(1)} fusion(bf16[2048,128]{1,0:T(8,128)(2,1)S(1)} %dynamic-slice_bitcast_fusion.4, s32[1024]{0:T(1024)S(1)} %broadcast_clamp_fusion.2), kind=kCustom, calls=%fused_computation.clone.clone.1 | custom fusion | bytes 528384 | tf_op jit(solution)/shard_map/while/body/eval_jaxpr/jit(_take)/gather | solution.py:70
  120.3 2.8 %gather_fusion.1 = s32[1024,8]{1,0:T(8,128)S(1)} fusion(s32[2048,8]{1,0:T(8,128)S(1)} %dynamic-slice_bitcast_fusion.5, s32[1024]{0:T(1024)S(1)} %broadcast_clamp_fusion.2), kind=kCustom, calls=%fused_computation.1.clone.clone.1 | custom fusion | bytes 69632 | tf_op jit(solution)/shard_map/while/body/eval_jaxpr/jit(_take)/gather | solution.py:71
  126.0 3.2 %gather_fusion = bf16[1024,128]{1,0:T(8,128)(2,1)S(1)} fusion(bf16[2048,128]{1,0:T(8,128)(2,1)S(1)} %dynamic-slice_bitcast_fusion.4, s32[1024]{0:T(1024)S(1)} %broadcast_clamp_fusion.2), kind=kCustom, calls=%fused_computation.clone.clone.1 | custom fusion | bytes 528384 | tf_op jit(solution)/shard_map/while/body/eval_jaxpr/jit(_take)/gather | solution.py:70
  132.3 2.8 %gather_fusion.1 = s32[1024,8]{1,0:T(8,128)S(1)} fusion(s32[2048,8]{1,0:T(8,128)S(1)} %dynamic-slice_bitcast_fusion.5, s32[1024]{0:T(1024)S(1)} %broadcast_clamp_fusion.2), kind=kCustom, calls=%fused_computation.1.clone.clone.1 | custom fusion | bytes 69632 | tf_op jit(solution)/shard_map/while/body/eval_jaxpr/jit(_take)/gather | solution.py:71
  138.0 3.2 %gather_fusion = bf16[1024,128]{1,0:T(8,128)(2,1)S(1)} fusion(bf16[2048,128]{1,0:T(8,128)(2,1)S(1)} %dynamic-slice_bitcast_fusion.4, s32[1024]{0:T(1024)S(1)} %broadcast_clamp_fusion.2), kind=kCustom, calls=%fused_computation.clone.clone.1 | custom fusion | bytes 528384 | tf_op jit(solution)/shard_map/while/body/eval_jaxpr/jit(_take)/gather | solution.py:70
  144.4 2.8 %gather_fusion.1 = s32[1024,8]{1,0:T(8,128)S(1)} fusion(s32[2048,8]{1,0:T(8,128)S(1)} %dynamic-slice_bitcast_fusion.5, s32[1024]{0:T(1024)S(1)} %broadcast_clamp_fusion.2), kind=kCustom, calls=%fused_computation.1.clone.clone.1 | custom fusion | bytes 69632 | tf_op jit(solution)/shard_map/while/body/eval_jaxpr/jit(_take)/gather | solution.py:71
  150.1 3.2 %gather_fusion = bf16[1024,128]{1,0:T(8,128)(2,1)S(1)} fusion(bf16[2048,128]{1,0:T(8,128)(2,1)S(1)} %dynamic-slice_bitcast_fusion.4, s32[1024]{0:T(1024)S(1)} %broadcast_clamp_fusion.2), kind=kCustom, calls=%fused_computation.clone.clone.1 | custom fusion | bytes 528384 | tf_op jit(solution)/shard_map/while/body/eval_jaxpr/jit(_take)/gather | solution.py:70
  156.4 2.8 %gather_fusion.1 = s32[1024,8]{1,0:T(8,128)S(1)} fusion(s32[2048,8]{1,0:T(8,128)S(1)} %dynamic-slice_bitcast_fusion.5, s32[1024]{0:T(1024)S(1)} %broadcast_clamp_fusion.2), kind=kCustom, calls=%fused_computation.1.clone.clone.1 | custom fusion | bytes 69632 | tf_op jit(solution)/shard_map/while/body/eval_jaxpr/jit(_take)/gather | solution.py:71
  162.1 3.2 %gather_fusion = bf16[1024,128]{1,0:T(8,128)(2,1)S(1)} fusion(bf16[2048,128]{1,0:T(8,128)(2,1)S(1)} %dynamic-slice_bitcast_fusion.4, s32[1024]{0:T(1024)S(1)} %broadcast_clamp_fusion.2), kind=kCustom, calls=%fused_computation.clone.clone.1 | custom fusion | bytes 528384 | tf_op jit(solution)/shard_map/while/body/eval_jaxpr/jit(_take)/gather | solution.py:70
  168.5 2.8 %gather_fusion.1 = s32[1024,8]{1,0:T(8,128)S(1)} fusion(s32[2048,8]{1,0:T(8,128)S(1)} %dynamic-slice_bitcast_fusion.5, s32[1024]{0:T(1024)S(1)} %broadcast_clamp_fusion.2), kind=kCustom, calls=%fused_computation.1.clone.clone.1 | custom fusion | bytes 69632 | tf_op jit(solution)/shard_map/while/body/eval_jaxpr/jit(_take)/gather | solution.py:71
  174.2 3.2 %gather_fusion = bf16[1024,128]{1,0:T(8,128)(2,1)S(1)} fusion(bf16[2048,128]{1,0:T(8,128)(2,1)S(1)} %dynamic-slice_bitcast_fusion.4, s32[1024]{0:T(1024)S(1)} %broadcast_clamp_fusion.2), kind=kCustom, calls=%fused_computation.clone.clone.1 | custom fusion | bytes 528384 | tf_op jit(solution)/shard_map/while/body/eval_jaxpr/jit(_take)/gather | solution.py:70
  180.5 2.8 %gather_fusion.1 = s32[1024,8]{1,0:T(8,128)S(1)} fusion(s32[2048,8]{1,0:T(8,128)S(1)} %dynamic-slice_bitcast_fusion.5, s32[1024]{0:T(1024)S(1)} %broadcast_clamp_fusion.2), kind=kCustom, calls=%fused_computation.1.clone.clone.1 | custom fusion | bytes 69632 | tf_op jit(solution)/shard_map/while/body/eval_jaxpr/jit(_take)/gather | solution.py:71
  186.2 3.2 %gather_fusion = bf16[1024,128]{1,0:T(8,128)(2,1)S(1)} fusion(bf16[2048,128]{1,0:T(8,128)(2,1)S(1)} %dynamic-slice_bitcast_fusion.4, s32[1024]{0:T(1024)S(1)} %broadcast_clamp_fusion.2), kind=kCustom, calls=%fused_computation.clone.clone.1 | custom fusion | bytes 528384 | tf_op jit(solution)/shard_map/while/body/eval_jaxpr/jit(_take)/gather | solution.py:70
  190.7 3.3 %all-to-all-start.1 = ((s32[1,8,1024]{2,0,1:T(1,128)}), s32[1,8,1024]{2,0,1:T(1,128)S(1)}, u32[]{:S(2)}, u32[]{:S(2)}) async-start(s32[1,8,1024]{2,0,1:T(1,128)} %broadcast_in_dim.94), calls=%async_computation.1 | async-start | bytes 65536 | tf_op jit(solution)/shard_map/all_to_all | solution.py:93
  195.2 2.1 reduce.1
  198.3 3.4 %all-to-all-start = ((bf16[4,2,16384]{2,1,0:T(2,128)(2,1)}), bf16[4,2,16384]{2,1,0:T(2,128)(2,1)S(1)}, u32[]{:S(2)}, u32[]{:S(2)}) async-start(bf16[4,2,16384]{2,1,0:T(2,128)(2,1)} %reshape.97), calls=%async_computation | async-start | bytes 524288 | tf_op jit(solution)/shard_map/all_to_all | solution.py:92
  203.5 4.2 %all-to-all-done = bf16[4,2,16384]{2,1,0:T(2,128)(2,1)S(1)} async-done(((bf16[4,2,16384]{2,1,0:T(2,128)(2,1)}), bf16[4,2,16384]{2,1,0:T(2,128)(2,1)S(1)}, u32[]{:S(2)}, u32[]{:S(2)}) %all-to-all-start) | async-done | bytes 262176 | tf_op jit(solution)/shard_map/all_to_all | solution.py:92
  210.8 34.7 %all-reduce.2 = (f32[2,16,256]{2,1,0:T(8,128)S(1)}, f32[2,256]{1,0:T(2,128)S(1)}) all-reduce(f32[2,16,256]{2,1,0:T(8,128)S(1)} %pad_maximum_fusion, f32[2,256]{1,0:T(2,128)S(1)} %pad_maximum_fusion.1), channel_id=1, replica_groups=mesh['wide'=8,'sub'=4] {'wide'}, use_global_device_ids=true, to_apply=%region_5.6 | all-reduce | flops 8704 | bytes 69632 | tf_op jit(solution)/shard_map/psum | solution.py:108
  (134 shorter events, 76.7 us)
Async XLA Ops:
  7.2 186.8 %copy-start = (bf16[128,128]{1,0:T(8,128)(2,1)S(1)}, bf16[128,128]{1,0:T(8,128)(2,1)}, u32[]{:S(2)}) copy-start(bf16[128,128]{1,0:T(8,128)(2,1)} %param.11) | copy-start | bytes 98308
  7.2 86.3 %all-gather.3.cloned.1.call-start = ((), (), s32[]{:S(2)}) async-start(), calls=%async_computation.2 | async-start | bytes 4718592 | tf_op jit(solution)/shard_map/all_gather | solution.py:81
  7.9 45.9 %collective-permute-start = (s32[1,2048,8]{1,2,0:T(8,128)}, s32[1,2048,8]{1,2,0:T(8,128)S(1)}, u32[]{:S(2)}, u32[]{:S(2)}) collective-permute-start(s32[1,2048,8]{1,2,0:T(8,128)} %bitcast.58), channel_id=1, source_target_pairs={{0,4},{4,8},{8,12},{12,16},{16,20},{20,24},{24,28},{28,0},{1,5},{5... | collective-permute-start | bytes 196616 | tf_op jit(solution)/shard_map/ppermute | solution.py:19
  14.9 40.7 %collective-permute-start.1 = (s32[1,2048,8]{1,2,0:T(8,128)}, s32[1,2048,8]{1,2,0:T(8,128)S(1)}, u32[]{:S(2)}, u32[]{:S(2)}) collective-permute-start(s32[1,2048,8]{1,2,0:T(8,128)} %bitcast.59), channel_id=1, source_target_pairs={{0,28},{4,0},{8,4},{12,8},{16,12},{20,16},{24,20},{28,24},{1,29},{... | collective-permute-start | bytes 196616 | tf_op jit(solution)/shard_map/ppermute | solution.py:24
  54.2 9.0 %collective-permute-start.2 = (s32[1,2048,8]{1,2,0:T(8,128)S(1)}, s32[1,2048,8]{1,2,0:T(8,128)S(1)}, u32[]{:S(2)}, u32[]{:S(2)}) collective-permute-start(s32[1,2048,8]{1,2,0:T(8,128)S(1)} %collective-permute-done), channel_id=1, source_target_pairs={{0,4},{4,8},{8,12},{12,16},{16,20},{20,24},{24,28},{28,0},{1,5},{5... | collective-permute-start | bytes 196616 | tf_op jit(solution)/shard_map/ppermute | solution.py:19
  55.9 7.7 %collective-permute-start.3 = (s32[1,2048,8]{1,2,0:T(8,128)S(1)}, s32[1,2048,8]{1,2,0:T(8,128)S(1)}, u32[]{:S(2)}, u32[]{:S(2)}) collective-permute-start(s32[1,2048,8]{1,2,0:T(8,128)S(1)} %collective-permute-done.1), channel_id=1, source_target_pairs={{0,28},{4,0},{8,4},{12,8},{16,12},{20,16},{24,20},{28,24},{1,29},{... | collective-permute-start | bytes 196616 | tf_op jit(solution)/shard_map/ppermute | solution.py:24
  63.5 8.8 %collective-permute-start.4 = (s32[1,2048,8]{1,2,0:T(8,128)S(1)}, s32[1,2048,8]{1,2,0:T(8,128)S(1)}, u32[]{:S(2)}, u32[]{:S(2)}) collective-permute-start(s32[1,2048,8]{1,2,0:T(8,128)S(1)} %collective-permute-done.2), channel_id=1, source_target_pairs={{0,4},{4,8},{8,12},{12,16},{16,20},{20,24},{24,28},{28,0},{1,5},{5... | collective-permute-start | bytes 196616 | tf_op jit(solution)/shard_map/ppermute | solution.py:19
  63.9 8.8 %collective-permute-start.5 = (s32[1,2048,8]{1,2,0:T(8,128)S(1)}, s32[1,2048,8]{1,2,0:T(8,128)S(1)}, u32[]{:S(2)}, u32[]{:S(2)}) collective-permute-start(s32[1,2048,8]{1,2,0:T(8,128)S(1)} %collective-permute-done.3), channel_id=1, source_target_pairs={{0,28},{4,0},{8,4},{12,8},{16,12},{20,16},{24,20},{28,24},{1,29},{... | collective-permute-start | bytes 196616 | tf_op jit(solution)/shard_map/ppermute | solution.py:24
  72.6 7.0 %collective-permute-start.6 = (s32[1,2048,8]{1,2,0:T(8,128)S(1)}, s32[1,2048,8]{1,2,0:T(8,128)S(1)}, u32[]{:S(2)}, u32[]{:S(2)}) collective-permute-start(s32[1,2048,8]{1,2,0:T(8,128)S(1)} %collective-permute-done.4), channel_id=1, source_target_pairs={{0,4},{4,8},{8,12},{12,16},{16,20},{20,24},{24,28},{28,0},{1,5},{5... | collective-permute-start | bytes 196616 | tf_op jit(solution)/shard_map/ppermute | solution.py:19
  190.7 7.5 %all-to-all-start.1 = ((s32[1,8,1024]{2,0,1:T(1,128)}), s32[1,8,1024]{2,0,1:T(1,128)S(1)}, u32[]{:S(2)}, u32[]{:S(2)}) async-start(s32[1,8,1024]{2,0,1:T(1,128)} %broadcast_in_dim.94), calls=%async_computation.1 | async-start | bytes 65536 | tf_op jit(solution)/shard_map/all_to_all | solution.py:93
  198.3 9.4 %all-to-all-start = ((bf16[4,2,16384]{2,1,0:T(2,128)(2,1)}), bf16[4,2,16384]{2,1,0:T(2,128)(2,1)S(1)}, u32[]{:S(2)}, u32[]{:S(2)}) async-start(bf16[4,2,16384]{2,1,0:T(2,128)(2,1)} %reshape.97), calls=%async_computation | async-start | bytes 524288 | tf_op jit(solution)/shard_map/all_to_all | solution.py:92
  208.0 38.2 %copy-start.1 = (bf16[1,128,1024]{2,1,0:T(8,128)(2,1)}, bf16[1,128,1024]{2,1,0:T(8,128)(2,1)S(1)}, u32[]{:S(2)}) copy-start(bf16[1,128,1024]{2,1,0:T(8,128)(2,1)S(1)} %copy.28) | copy-start | bytes 786436
Sparse Core Ops, SparseCore 0:
  10.1 83.3 all-gather.2
